TPU v7x, 32 devices: a whole 2x2x4 slice. The times are simulated.
32 devices in a mesh: dp: 2 (over y), seq: 4 (over z), section: 4 (over x, core).
Axes of the slice: x: 2, y: 2, z: 4, core: 2. Of those that a mesh axis runs over, the one named last changes fastest.
Arguments:
- signal: bfloat16 [2, 2560, 1280], P('dp', 'seq'), may hold values from -6 to 6
- kernel: bfloat16 [1536, 5, 1280], P('section'), may hold values from -0.078125 to 0.078125
- trunk_grad: bfloat16 [2, 1280, 1536], P('dp', ('seq', 'section')), may hold values from -6 to 6
Outputs:
- weight_grad: float32 [1536, 5, 1280], P(('section', 'seq'))
- input_grad: bfloat16 [2, 1280, 2560], P('dp', 'section', 'seq')
All inputs are finite; a program needn't handle non-finite values.
Results may differ from a plain program's by a relative error of at most 0.019.
Values may be sent and summed in bfloat16 or wider, within the bound.
A program may use at most 64 MiB of HBM per device.

v0:
```python
import jax
import jax.numpy as jnp
from jax import lax
from jax.sharding import PartitionSpec as P


def extended(block, sides, width):
    for axis, dim in sides:
        count = lax.axis_size(axis)
        forward = [(i, i + 1) for i in range(count - 1)]
        backward = [(target, source) for source, target in forward]
        low = lax.ppermute(
            lax.slice_in_dim(block, block.shape[dim] - width, None, axis=dim), axis, forward
        )
        high = lax.ppermute(lax.slice_in_dim(block, 0, width, axis=dim), axis, backward)
        block = jnp.concatenate([low, block, high], axis=dim)
    return block


def gelu_slope(values):
    normal_cdf = 0.5 * (1.0 + jax.scipy.special.erf(values * 0.7071067811865476))
    density = jnp.exp(-0.5 * values * values) * 0.3989422804014327
    return normal_cdf + values * density


def convolve(padded, kernel, out_rows):
    linear = jnp.einsum(
        "lc,oc->lo", padded[0:out_rows], kernel[:, 0, :], preferred_element_type=jnp.float32
    )
    for offset in range(1, kernel.shape[1]):
        linear = linear + jnp.einsum(
            "lc,oc->lo",
            padded[offset : offset + out_rows],
            kernel[:, offset, :],
            preferred_element_type=jnp.float32,
        )
    return linear


def shards(signal, kernel, trunk_grad):
    local_signal = signal[0]
    length = local_signal.shape[0]
    taps_count = kernel.shape[1]
    pooled = lax.all_to_all(trunk_grad, "section", split_axis=2, concat_axis=1, tiled=True)[0]
    padded = extended(local_signal, (("seq", 0),), 2)
    linear = convolve(padded, kernel, length)
    grad_hidden = 0.5 * jnp.repeat(pooled.astype(jnp.float32), 2, axis=0)
    grad_pre = (grad_hidden * gelu_slope(linear)).astype(jnp.bfloat16)
    grad_ext = extended(grad_pre, (("seq", 0),), 2)
    grad_middle = grad_ext[2 : 2 + length]
    taps = []
    for offset in range(taps_count):
        taps.append(
            jnp.einsum(
                "lo,lc->oc",
                grad_middle,
                padded[offset : offset + length],
                preferred_element_type=jnp.float32,
            )
        )
    weight_rows = lax.psum_scatter(
        jnp.stack(taps, axis=1).astype(jnp.bfloat16), "seq", scatter_dimension=0, tiled=True
    )
    weight_grad = lax.psum(weight_rows, "dp").astype(jnp.float32)
    summed = jnp.einsum(
        "lo,oc->cl", grad_ext[4 : 4 + length], kernel[:, 0, :], preferred_element_type=jnp.float32
    )
    for offset in range(1, taps_count):
        summed = summed + jnp.einsum(
            "lo,oc->cl",
            grad_ext[4 - offset : 4 - offset + length],
            kernel[:, offset, :],
            preferred_element_type=jnp.float32,
        )
    input_rows = lax.psum_scatter(
        summed.astype(jnp.bfloat16), "section", scatter_dimension=0, tiled=True
    )
    return (weight_grad, input_rows[None])


def solution(mesh):
    return jax.shard_map(
        shards,
        mesh=mesh,
        in_specs=(
            P("dp", "seq", None),
            P("section", None, None),
            P("dp", ("seq", "section"), None),
        ),
        out_specs=(P(("section", "seq"), None, None), P("dp", "section", "seq")),
        check_vma=False,
    )
```

profile of v0, /device:TPU:0, one launch (start us, length us, event | category | flops | bytes accessed | tf_op | source)
XLA Modules:
  0.0 237.2 jit_solution(3593745653070682737)
XLA Ops:
  7.2 0.0 copy-start
  7.2 0.9 slice_bitcast_fusion.1
  8.1 4.9 %collective-permute-start = (bf16[2,1280]{1,0:T(2,128)(2,1)S(1)}, bf16[2,1280]{1,0:T(2,128)(2,1)S(1)}, u32[]{:S(2)}, u32[]{:S(2)}) collective-permute-start(bf16[2,1280]{1,0:T(2,128)(2,1)S(1)} %get-tuple-element.12), channel_id=1, source_target_pairs={{0,4},{4,8},{8,12},{1,5},{5,9},{9,13},{2,6},{6,10},{10,14},{3,7},{... | collective-permute-start | bytes 15368 | tf_op jit(solution)/shard_map/ppermute | solution.py:12
  13.0 1.3 collective-permute-start.1
  14.3 2.1 copy.13
  16.4 0.5 broadcast.19
  16.9 8.8 %reduce = bf16[1536,80]{1,0:T(8,128)(2,1)S(1)} reduce(bf16[1536,1,80]{2,1,0:T(2,128)(2,1)S(1)} %bitcast.70, bf16[]{:T(256)} %broadcast.19), dimensions={1}, to_apply=%bitcast.62.reduce_sub_computation | reduce | bytes 491522
  25.8 1.4 reshape.18
  27.1 3.4 %all-to-all-start = ((bf16[4,2,15360]{2,1,0:T(2,128)(2,1)}), bf16[4,2,15360]{2,1,0:T(2,128)(2,1)S(1)}, u32[]{:S(2)}, u32[]{:S(2)}) async-start(bf16[4,2,15360]{2,1,0:T(2,128)(2,1)} %reshape.18), calls=%async_computation | async-start | bytes 491520 | tf_op jit(solution)/shard_map/all_to_all | solution.py:44
  30.5 0.2 reduce-scatter.5.cloned.1.call-start
  30.8 0.0 copy-done
  30.8 2.2 fusion.33
  33.0 0.0 collective-permute-done
  33.0 2.2 fusion.18
  35.3 3.2 %fusion.17 = f32[640,384]{1,0:T(8,128)} fusion(f32[640,384]{1,0:T(8,128)S(1)} %fusion.33, f32[640,384]{1,0:T(8,128)S(1)} %fusion.18, bf16[384,5,1280]{2,0,1:T(8,128)(2,1)} %param.4, bf16[2,1280]{1,0:T(2,128)(2,1)S(1)} %collective-permute-done, bf16[640,1280]{1,0:T(8,128)(2,1)S(1)} %bitcast.77), kind=kOutput, calls=%fused_computation.33 | convolution fusion | flops 632913920 | bytes 5575680 | tf_op jit(solution)/shard_map/lc,oc->lo/dot_general | solution.py:27
  38.5 0.0 collective-permute-done.1
  38.5 3.2 %fusion.19 = f32[640,384]{1,0:T(8,128)} fusion(bf16[2,1280]{1,0:T(2,128)(2,1)S(1)} %collective-permute-done.1, bf16[640,1280]{1,0:T(8,128)(2,1)S(1)} %bitcast.78, bf16[384,5,1280]{2,0,1:T(8,128)(2,1)} %param.4), kind=kOutput, calls=%fused_computation.35 | convolution fusion | flops 632422400 | bytes 3609600 | tf_op jit(solution)/shard_map/lc,oc->lo/dot_general | solution.py:31
  41.6 0.0 all-to-all-done
  41.6 0.8 reshape.19
  42.4 0.5 copy.14
  43.0 0.2 mul.47
  43.2 0.3 broadcast_in_dim.6
  43.5 0.7 mul.50
  44.2 0.0 copy-start.1
  44.2 3.7 %fusion.25 = bf16[640,384]{1,0:T(8,128)(2,1)S(1)} fusion(f32[640,384]{1,0:T(8,128)S(1)} %mul.50, f32[640,384]{1,0:T(8,128)} %fusion.19, f32[640,384]{1,0:T(8,128)} %fusion.17, bf16[384,5,1280]{2,0,1:T(8,128)(2,1)} %param.4, bf16[640,1280]{1,0:T(8,128)(2,1)} %bitcast.75, bf16[2,1280]{1,0:T(2,128)(2,1)S(1)} %collective-permute-done.1), kind=kOutput, calls=%fused_computation.41 | convolution fusion | flops 635371520 | bytes 6067200 | tf_op jit(solution)/shard_map/lc,oc->lo/dot_general | solution.py:31
  48.0 0.0 copy-done.1
  48.0 1.9 fusion.5
  49.9 2.0 fusion.7
  51.9 1.9 fusion.9
  53.9 1.9 fusion.11
  55.8 1.9 fusion.13
  57.7 0.0 reduce-scatter.5.cloned.1.call-update
  57.8 0.0 reduce-scatter.7.cloned.1.call-start
  57.8 4.6 %collective-permute-start.3 = (bf16[2,384]{1,0:T(2,128)(2,1)S(1)}, bf16[2,384]{1,0:T(2,128)(2,1)S(1)}, u32[]{:S(2)}, u32[]{:S(2)}) collective-permute-start(bf16[2,384]{1,0:T(2,128)(2,1)S(1)} %get-tuple-element.15), channel_id=1, source_target_pairs={{0,4},{4,8},{8,12},{1,5},{5,9},{9,13},{2,6},{6,10},{10,14},{3,7},{... | collective-permute-start | bytes 4616 | tf_op jit(solution)/shard_map/ppermute | solution.py:12
  62.4 2.2 fusion.31
  64.6 1.5 collective-permute-start.2
  66.1 0.0 collective-permute-done.3
  66.1 2.5 %fusion.26 = f32[640,1280]{1,0:T(8,128)S(1)} fusion(bf16[384,5,1280]{2,0,1:T(8,128)(2,1)} %param.4, bf16[640,384]{1,0:T(8,128)(2,1)S(1)} %fusion.25, bf16[2,384]{1,0:T(2,128)(2,1)S(1)} %collective-permute-done.3), kind=kOutput, calls=%fused_computation.42 | convolution fusion | flops 630128640 | bytes 4752896 | tf_op jit(solution)/shard_map/lo,oc->cl/dot_general | solution.py:69
  68.6 1.4 collective-permute-done.2
  70.1 2.2 fusion.35
  72.3 2.2 fusion.1
  74.5 2.2 fusion.3
  76.8 2.2 copy.17
  79.0 0.0 reduce-scatter.7.cloned.1.call-update
  79.0 0.0 all-reduce.2.cloned.1.call-start
  79.1 69.9 %reduce-scatter.5.cloned.1.call-done = bf16[96,5,1280]{2,0,1:T(8,128)(2,1)} async-done(((bf16[384,5,1280]{2,0,1:T(8,128)(2,1)}), bf16[96,5,1280]{2,0,1:T(8,128)(2,1)}) %reduce-scatter.5.cloned.1.call-update) | async-done | bytes 1228816 | tf_op jit(solution)/shard_map/reduce_scatter | solution.py:61
  149.0 0.0 all-reduce.2.cloned.1.call-update
  149.0 32.4 %reduce-scatter.7.cloned.1.call-done = bf16[320,640]{1,0:T(8,128)(2,1)} async-done(((bf16[1280,640]{1,0:T(8,128)(2,1)}), bf16[320,640]{1,0:T(8,128)(2,1)}) %reduce-scatter.7.cloned.1.call-update) | async-done | bytes 409616
  181.4 1.3 copy.18
  182.6 1.0 copy.16
  183.6 44.1 %all-reduce.2.cloned.1.call-done = bf16[96,5,1280]{2,0,1:T(8,128)(2,1)} async-done(((bf16[96,5,1280]{2,0,1:T(8,128)(2,1)}), bf16[96,5,1280]{2,0,1:T(8,128)(2,1)}) %all-reduce.2.cloned.1.call-update) | async-done | bytes 1228816 | tf_op jit(solution)/shard_map/psum | solution.py:64
  227.7 2.9 %convert_element_type.16 = f32[96,5,1280]{2,0,1:T(8,128)} convert(bf16[96,5,1280]{2,0,1:T(8,128)(2,1)} %all-reduce.2.cloned.1.call-done) | non-fusion elementwise | flops 614400 | bytes 3686400 | tf_op jit(solution)/shard_map/convert_element_type | solution.py:64
  (3 shorter events, 0.1 us)
Async XLA Ops:
  7.2 23.6 %copy-start = (bf16[1,640,1280]{2,1,0:T(8,128)(2,1)S(1)}, bf16[1,640,1280]{2,1,0:T(8,128)(2,1)}, u32[]{:S(2)}) copy-start(bf16[1,640,1280]{2,1,0:T(8,128)(2,1)} %param.3) | copy-start | bytes 4915204
  8.1 25.0 %collective-permute-start = (bf16[2,1280]{1,0:T(2,128)(2,1)S(1)}, bf16[2,1280]{1,0:T(2,128)(2,1)S(1)}, u32[]{:S(2)}, u32[]{:S(2)}) collective-permute-start(bf16[2,1280]{1,0:T(2,128)(2,1)S(1)} %get-tuple-element.12), channel_id=1, source_target_pairs={{0,4},{4,8},{8,12},{1,5},{5,9},{9,13},{2,6},{6,10},{10,14},{3,7},{... | collective-permute-start | bytes 15368 | tf_op jit(solution)/shard_map/ppermute | solution.py:12
  13.0 25.5 %collective-permute-start.1 = (bf16[2,1280]{1,0:T(2,128)(2,1)S(1)}, bf16[2,1280]{1,0:T(2,128)(2,1)S(1)}, u32[]{:S(2)}, u32[]{:S(2)}) collective-permute-start(bf16[2,1280]{1,0:T(2,128)(2,1)S(1)} %get-tuple-element.13), channel_id=1, source_target_pairs={{4,0},{8,4},{12,8},{5,1},{9,5},{13,9},{6,2},{10,6},{14,10},{7,3},{... | collective-permute-start | bytes 15368 | tf_op jit(solution)/shard_map/ppermute | solution.py:15
  27.1 14.5 %all-to-all-start = ((bf16[4,2,15360]{2,1,0:T(2,128)(2,1)}), bf16[4,2,15360]{2,1,0:T(2,128)(2,1)S(1)}, u32[]{:S(2)}, u32[]{:S(2)}) async-start(bf16[4,2,15360]{2,1,0:T(2,128)(2,1)} %reshape.18), calls=%async_computation | async-start | bytes 491520 | tf_op jit(solution)/shard_map/all_to_all | solution.py:44
  30.5 118.4 %reduce-scatter.5.cloned.1.call-start = ((), (), s32[]{:S(2)}) async-start(), calls=%async_computation.3 | async-start | bytes 6144000 | tf_op jit(solution)/shard_map/reduce_scatter | solution.py:61
  44.2 3.8 %copy-start.1 = (bf16[1,640,1280]{2,1,0:T(8,128)(2,1)S(1)}, bf16[1,640,1280]{2,1,0:T(8,128)(2,1)}, u32[]{:S(2)}) copy-start(bf16[1,640,1280]{2,1,0:T(8,128)(2,1)} %param.3) | copy-start | bytes 4915204
  57.8 123.6 %reduce-scatter.7.cloned.1.call-start = ((), (), s32[]{:S(2)}) async-start(), calls=%async_computation.5 | async-start | bytes 2048000
  57.8 8.3 %collective-permute-start.3 = (bf16[2,384]{1,0:T(2,128)(2,1)S(1)}, bf16[2,384]{1,0:T(2,128)(2,1)S(1)}, u32[]{:S(2)}, u32[]{:S(2)}) collective-permute-start(bf16[2,384]{1,0:T(2,128)(2,1)S(1)} %get-tuple-element.15), channel_id=1, source_target_pairs={{0,4},{4,8},{8,12},{1,5},{5,9},{9,13},{2,6},{6,10},{10,14},{3,7},{... | collective-permute-start | bytes 4616 | tf_op jit(solution)/shard_map/ppermute | solution.py:12
  64.6 5.5 %collective-permute-start.2 = (bf16[2,384]{1,0:T(2,128)(2,1)S(1)}, bf16[2,384]{1,0:T(2,128)(2,1)S(1)}, u32[]{:S(2)}, u32[]{:S(2)}) collective-permute-start(bf16[2,384]{1,0:T(2,128)(2,1)S(1)} %get-tuple-element.14), channel_id=1, source_target_pairs={{4,0},{8,4},{12,8},{5,1},{9,5},{13,9},{6,2},{10,6},{14,10},{7,3},{... | collective-permute-start | bytes 4616 | tf_op jit(solution)/shard_map/ppermute | solution.py:15
  79.0 148.7 %all-reduce.2.cloned.1.call-start = ((), (), s32[]{:S(2)}) async-start(), calls=%async_computation.4 | async-start | bytes 2457600 | tf_op jit(solution)/shard_map/psum | solution.py:64
Sparse Core Ops, SparseCore 0:
  57.9 91.0 reduce-scatter.4
  152.3 29.0 reduce-scatter.6
  183.7 43.9 all-reduce.1
where the time goes:
time: 238 us; the launch traced here: 237 us
  waiting for transfers between devices  148 us (62%)
  matrix products  35.7 us (15%)
  starting transfers between devices  16 us (7%)
  between operations  14 us (6%)
  local copies, waits for them, and re-layouts  11.8 us (5%)
  other arithmetic  11.8 us (5%)
    reduce_scatter x1, waiting for transfers between devices, shards(): lax.psum_scatter(jnp.stack(taps, axis=1).astype(jnp.bfloat16), 'seq', sca...  69.9 us
    psum x1, waiting for transfers between devices, shards(): weight_grad = lax.psum(weight_rows, 'dp').astype(jnp.float32)  44.1 us
    unnamed x4, waiting for transfers between devices  32.4 us
    dot_general x4, matrix products, convolve(): jnp.einsum('lc,oc->lo', padded[offset:offset + out_rows], kernel[:, offse...  11.4 us
    dot_general x5, matrix products, shards(): jnp.einsum('lo,lc->oc', grad_middle, padded[offset:offset + length], pref...  9.74 us
    ppermute x2, starting transfers between devices, extended(): lax.ppermute(lax.slice_in_dim(block, block.shape[dim] - width, None, axis...  9.5 us
    unnamed x11, local copies, waits for them, and re-layouts  9.23 us
    dot_general x4, matrix products, shards(): jnp.einsum('lo,oc->cl', grad_ext[4 - offset:4 - offset + length], kernel[...  9.16 us
  transfers between devices with their start and end apart: 8, of which 4 were waited for; matrix products, arithmetic and copies ran while one was open for 17% of the time, Pallas kernels for 0%

commit v1 on v0

v1 whole, which is shorter than its diff:
```python
import jax
import jax.numpy as jnp
from jax import lax
from jax.sharding import PartitionSpec as P


def edges(block, axis, width):
    count = lax.axis_size(axis)
    forward = [(i, i + 1) for i in range(count - 1)]
    backward = [(target, source) for source, target in forward]
    low = lax.ppermute(block[-width:], axis, forward)
    high = lax.ppermute(block[:width], axis, backward)
    return jnp.concatenate([low, block, high], axis=0)


def gelu_slope(values):
    normal_cdf = 0.5 * (1.0 + jax.scipy.special.erf(values * 0.7071067811865476))
    density = jnp.exp(-0.5 * values * values) * 0.3989422804014327
    return normal_cdf + values * density


def shards(signal, kernel, trunk_grad):
    n_dp = lax.axis_size("dp")
    n_section = lax.axis_size("section")
    me = lax.axis_index("dp")
    local = signal[0]
    length, c_in = local.shape
    c_out, taps_count, _ = kernel.shape
    width = taps_count // 2
    share = c_in // n_dp
    flat = jnp.transpose(kernel, (1, 0, 2)).reshape(taps_count * c_out, c_in)

    rows = trunk_grad.shape[1]
    trunk = jnp.transpose(trunk_grad[0].reshape(rows, n_section, c_out), (1, 0, 2))
    pooled = lax.all_to_all(trunk, "section", split_axis=0, concat_axis=0).reshape(
        n_section * rows, c_out
    )
    padded = edges(local, "seq", width)

    rings = [[(i, (i + step) % n_dp) for i in range(n_dp)] for step in range(n_dp)]

    def columns(owner):
        return lax.dynamic_slice_in_dim(padded, owner * share, share, axis=1)

    windows = [columns(me)]
    for step in range(1, n_dp):
        windows.append(lax.ppermute(columns((me + step) % n_dp), "dp", rings[step]))

    product = lax.dot_general(
        padded, flat, (((1,), (1,)), ((), ())), preferred_element_type=jnp.float32
    )
    linear = product[0:length, 0:c_out]
    for tap in range(1, taps_count):
        linear = linear + product[tap : tap + length, tap * c_out : (tap + 1) * c_out]
    grad_hidden = 0.5 * jnp.repeat(pooled.astype(jnp.float32), 2, axis=0)
    grad_pre = (grad_hidden * gelu_slope(linear)).astype(jnp.bfloat16)

    grads = [grad_pre]
    for step in range(1, n_dp):
        grads.append(lax.ppermute(grad_pre, "dp", rings[step]))
    grad_ext = edges(grad_pre, "seq", width)

    all_grads = jnp.concatenate(grads, axis=0)
    taps = []
    for tap in range(taps_count):
        window = jnp.concatenate([w[tap : tap + length] for w in windows], axis=0)
        taps.append(
            lax.dot_general(
                all_grads, window, (((0,), (0,)), ((), ())), preferred_element_type=jnp.float32
            ).astype(jnp.bfloat16)
        )
    partial = jnp.stack(taps, axis=1)
    weight_rows = lax.psum_scatter(partial, "seq", scatter_dimension=0, tiled=True)

    stacked = jnp.concatenate(
        [grad_ext[2 * width - tap : 2 * width - tap + length] for tap in range(taps_count)], axis=1
    )
    summed = lax.dot_general(
        flat, stacked, (((0,), (1,)), ((), ())), preferred_element_type=jnp.float32
    ).astype(jnp.bfloat16)
    input_rows = lax.psum_scatter(summed, "section", scatter_dimension=0, tiled=True)

    weight_grad = jnp.zeros(weight_rows.shape[:2] + (c_in,), jnp.float32)
    weight_grad = lax.dynamic_update_slice_in_dim(
        weight_grad, weight_rows.astype(jnp.float32), me * share, axis=2
    )
    for step in range(1, n_dp):
        other = lax.ppermute(weight_rows, "dp", rings[step])
        weight_grad = lax.dynamic_update_slice_in_dim(
            weight_grad, other.astype(jnp.float32), ((me - step) % n_dp) * share, axis=2
        )
    return (weight_grad, input_rows[None])


def solution(mesh):
    return jax.shard_map(
        shards,
        mesh=mesh,
        in_specs=(
            P("dp", "seq", None),
            P("section", None, None),
            P("dp", ("seq", "section"), None),
        ),
        out_specs=(P(("section", "seq"), None, None), P("dp", "section", "seq")),
        check_vma=False,
    )
```

time: 238 us -> 155 us (0.65)
  waiting for transfers between devices: 148 us -> 76.8 us
  matrix products: 35.7 us -> 19.3 us
  local copies, waits for them, and re-layouts: 11.8 us -> 17.6 us
  other arithmetic: 11.8 us -> 6.29 us
  starting transfers between devices: 16 us -> 19.9 us
    psum x1 -> x0, waiting for transfers between devices: 44.1 us -> none  [shards(): weight_grad = lax.psum(weight_rows, 'dp').astype(jnp.float32)]
    reduce_scatter x1, waiting for transfers between devices: 69.9 us -> 35.6 us  [shards(): lax.psum_scatter(partial, 'seq', scatter_dimension=0, tiled=True)]
    dot_general x15 -> x7, matrix products: 35.7 us -> 19.3 us  [the longest x1 8.04 us: shards(): lax.dot_general(padded, flat, (((1,), (1,)), ((), ())), preferred_element...]
    ppermute x4 -> x7, waiting for transfers between devices: 1.45 us -> 11.9 us  [the longest x1 9.28 us: shards(): grads.append(lax.ppermute(grad_pre, 'dp', rings[step]))]
    unnamed x1 -> x3, other arithmetic: 8.81 us -> 0.44 us
    ppermute x4 -> x7, starting transfers between devices: 12.3 us -> 16.5 us  [the longest x2 10.3 us: edges(): low = lax.ppermute(block[-width:], axis, forward)]
    unnamed x4 -> x3, waiting for transfers between devices: 32.4 us -> 29.3 us
    unnamed x11 -> x12, local copies, waits for them, and re-layouts: 9.23 us -> 7.36 us
  transfers between devices with their start and end apart: 8 -> 10, of which waited for: 4 -> 5; matrix products, arithmetic and copies ran while one was open for 17% -> 22% of each run, Pallas kernels for 0% -> 0%
where the time goes in v1:
time: 155 us; the launch traced here: 154 us
  waiting for transfers between devices  76.8 us (50%)
  starting transfers between devices  19.9 us (13%)
  matrix products  19.3 us (12%)
  local copies, waits for them, and re-layouts  17.6 us (11%)
  between operations  14.3 us (9%)
  other arithmetic  6.29 us (4%)
    reduce_scatter x1, waiting for transfers between devices, shards(): lax.psum_scatter(partial, 'seq', scatter_dimension=0, tiled=True)  35.6 us
    unnamed x3, waiting for transfers between devices  29.3 us
    ppermute x2, starting transfers between devices, edges(): low = lax.ppermute(block[-width:], axis, forward)  10.3 us
    ppermute x1, waiting for transfers between devices, shards(): grads.append(lax.ppermute(grad_pre, 'dp', rings[step]))  9.28 us
    dot_general x1, matrix products, shards(): lax.dot_general(padded, flat, (((1,), (1,)), ((), ())), preferred_element...  8.04 us
    unnamed x12, local copies, waits for them, and re-layouts  7.36 us
    dot_general x1, matrix products, shards(): lax.dot_general(flat, stacked, (((0,), (1,)), ((), ())), preferred_elemen...  6.23 us
    dot_general x5, matrix products, shards(): lax.dot_general(all_grads, window, (((0,), (0,)), ((), ())), preferred_el...  5.04 us
  transfers between devices with their start and end apart: 10, of which 5 were waited for; matrix products, arithmetic and copies ran while one was open for 22% of the time, Pallas kernels for 0%

profile of v1, /device:TPU:0, one launch (start us, length us, event | category | flops | bytes accessed | tf_op | source)
XLA Modules:
  0.0 154.2 jit_solution(947034816897265503)
XLA Ops:
  7.2 0.8 slice_bitcast_fusion.1
  7.9 4.9 %collective-permute-start = (bf16[2,1280]{1,0:T(2,128)(2,1)S(1)}, bf16[2,1280]{1,0:T(2,128)(2,1)S(1)}, u32[]{:S(2)}, u32[]{:S(2)}) collective-permute-start(bf16[2,1280]{1,0:T(2,128)(2,1)S(1)} %get-tuple-element.15), channel_id=1, source_target_pairs={{0,4},{4,8},{8,12},{1,5},{5,9},{9,13},{2,6},{6,10},{10,14},{3,7},{... | collective-permute-start | bytes 15368 | tf_op jit(solution)/shard_map/ppermute | solution.py:11
  12.9 1.3 collective-permute-start.1
  14.2 1.0 reshape_squeeze.3
  15.2 0.7 copy.9
  15.9 3.4 %all-to-all-start = ((bf16[4,80,384]{2,1,0:T(8,128)(2,1)}), bf16[4,80,384]{2,1,0:T(8,128)(2,1)S(1)}, u32[]{:S(2)}, u32[]{:S(2)}) async-start(bf16[4,80,384]{2,1,0:T(8,128)(2,1)} %copy.9), calls=%async_computation | async-start | bytes 491520 | tf_op jit(solution)/shard_map/all_to_all | solution.py:35
  19.3 0.0 reduce-scatter.5.cloned.1.call-start
  19.4 0.0 collective-permute-done
  19.4 0.0 collective-permute-done.1
  19.4 0.0 copy-start.2
  19.4 1.9 %pad_maximum_fusion = bf16[644,1280]{1,0:T(8,128)(2,1)S(1)} fusion(bf16[2,1280]{1,0:T(2,128)(2,1)S(1)} %collective-permute-done.1, bf16[640,1280]{1,0:T(8,128)(2,1)} %bitcast.39, bf16[2,1280]{1,0:T(2,128)(2,1)S(1)} %collective-permute-done), kind=kLoop, calls=%fused_computation.2 | loop fusion | flops 4945920 | bytes 3297280 | tf_op jit(solution)/shard_map/concatenate | solution.py:13
  21.3 1.0 constant_dynamic-slice_fusion.1
  22.3 1.6 %collective-permute-start.3 = (bf16[644,640]{1,0:T(8,128)(2,1)}, bf16[644,640]{1,0:T(8,128)(2,1)S(1)}, u32[]{:S(2)}, u32[]{:S(2)}) collective-permute-start(bf16[644,640]{1,0:T(8,128)(2,1)} %constant_dynamic-slice_fusion.1), channel_id=1, source_target_pairs={{0,16},{16,0},{1,17},{17,1},{2,18},{18,2},{3,19},{19,3},{4,20},{20... | collective-permute-start | bytes 2472968 | tf_op jit(solution)/shard_map/ppermute | solution.py:47
  23.9 0.0 copy-done.2
  23.9 8.0 %fusion.83 = f32[644,1920]{1,0:T(8,128)} fusion(bf16[1920,1280]{1,0:T(8,128)(2,1)} %bitcast.42, bf16[2,1280]{1,0:T(2,128)(2,1)S(1)} %collective-permute-done.1, bf16[640,1280]{1,0:T(8,128)(2,1)S(1)} %bitcast.40, bf16[2,1280]{1,0:T(2,128)(2,1)S(1)} %collective-permute-done), kind=kOutput, calls=%fused_computation.75 | convolution fusion | flops 3170334720 | bytes 11509760 | tf_op jit(solution)/shard_map/dot_general | solution.py:49
  31.9 0.0 all-to-all-done
  32.0 1.3 broadcast_in_dim.10
  33.2 2.9 %mul.52 = f32[640,384]{1,0:T(8,128)} reshape(f32[320,2,384]{2,1,0:T(2,128)} %broadcast_in_dim.10) | data formatting | bytes 1966080 | tf_op jit(solution)/shard_map/mul | solution.py:55
  36.1 3.5 %fusion.71 = bf16[640,384]{1,0:T(8,128)(2,1)S(1)} fusion(f32[640,384]{1,0:T(8,128)} %mul.52, f32[644,1920]{1,0:T(8,128)} %fusion.83), kind=kLoop, calls=%fused_computation.46 | loop fusion | flops 3440640 | bytes 6389760 | tf_op jit(solution)/shard_map/convert_element_type | solution.py:56
  39.6 0.6 collective-permute-start.2
  40.2 1.8 %fusion.84 = (bf16[640,640]{1,0:T(8,128)(2,1)S(1)}, bf16[640,640]{1,0:T(8,128)(2,1)S(1)}, bf16[640,640]{1,0:T(8,128)(2,1)S(1)}, bf16[640,640]{1,0:T(8,128)(2,1)S(1)}, bf16[640,640]{1,0:T(8,128)(2,1)S(1)}) fusion(bf16[644,1280]{1,0:T(8,128)(2,1)S(1)} %pad_maximum_fusion, s32[]{:T(128)S(6)} %add.62, s32[]{:T(128)S(6)} %select_n.21, s32[]{:T(128)S(6)} %add.60, ...), kind=kLoop, calls=%fused_computation.76 | loop fusion | bytes 8192020 | tf_op jit(solution)/shard_map/slice | solution.py:66
  42.0 1.9 %collective-permute-done.3 = bf16[644,640]{1,0:T(8,128)(2,1)S(1)} collective-permute-done((bf16[644,640]{1,0:T(8,128)(2,1)}, bf16[644,640]{1,0:T(8,128)(2,1)S(1)}, u32[]{:S(2)}, u32[]{:S(2)}) %collective-permute-start.3) | collective-permute-done | bytes 824352 | tf_op jit(solution)/shard_map/ppermute | solution.py:47
  43.8 0.7 fusion.85
  44.6 9.3 %collective-permute-done.2 = bf16[640,384]{1,0:T(8,128)(2,1)S(1)} collective-permute-done((bf16[640,384]{1,0:T(8,128)(2,1)S(1)}, bf16[640,384]{1,0:T(8,128)(2,1)S(1)}, u32[]{:S(2)}, u32[]{:S(2)}) %collective-permute-start.2) | collective-permute-done | bytes 491552 | tf_op jit(solution)/shard_map/ppermute | solution.py:60
  53.8 1.0 fusion.39
  54.8 1.0 fusion.45
  55.8 1.0 fusion.51
  56.8 1.0 fusion.57
  57.9 1.0 fusion.63
  58.9 0.0 copy-start
  58.9 1.4 copy-done
  60.3 0.0 reduce-scatter.5.cloned.1.call-update
  60.4 0.0 reduce-scatter.7.cloned.1.call-start
  60.4 1.3 collective-permute-start.5
  61.7 5.4 %collective-permute-start.6 = (bf16[2,384]{1,0:T(2,128)(2,1)S(1)}, bf16[2,384]{1,0:T(2,128)(2,1)S(1)}, u32[]{:S(2)}, u32[]{:S(2)}) collective-permute-start(bf16[2,384]{1,0:T(2,128)(2,1)S(1)} %get-tuple-element.22), channel_id=1, source_target_pairs={{0,4},{4,8},{8,12},{1,5},{5,9},{9,13},{2,6},{6,10},{10,14},{3,7},{... | collective-permute-start | bytes 4616 | tf_op jit(solution)/shard_map/ppermute | solution.py:11
  67.1 0.0 collective-permute-done.5
  67.1 0.1 fusion.75
  67.2 0.2 fusion.77
  67.4 0.1 constant_dynamic-update-slice_fusion
  67.5 0.7 collective-permute-done.6
  68.2 0.2 fusion.73
  68.3 0.2 fusion.76
  68.5 6.2 %fusion = bf16[1280,640]{0,1:T(8,128)(2,1)S(1)} fusion(bf16[640,1920]{1,0:T(8,128)(2,1)S(1)} %fusion.76, bf16[1920,1280]{1,0:T(8,128)(2,1)} %bitcast.43), kind=kOutput, calls=%fused_computation.1 | convolution fusion | flops 3146547200 | bytes 9011200 | tf_op jit(solution)/shard_map/dot_general | solution.py:78
  74.7 2.2 %copy.11 = bf16[1280,640]{1,0:T(8,128)(2,1)} copy(bf16[1280,640]{0,1:T(8,128)(2,1)S(1)} %fusion) | data formatting | bytes 3276800
  76.9 0.0 reduce-scatter.7.cloned.1.call-update
  77.0 35.6 %reduce-scatter.5.cloned.1.call-done = bf16[96,5,640]{2,0,1:T(8,128)(2,1)} async-done(((bf16[384,5,640]{2,0,1:T(8,128)(2,1)}), bf16[96,5,640]{2,0,1:T(8,128)(2,1)}) %reduce-scatter.5.cloned.1.call-update) | async-done | bytes 614416 | tf_op jit(solution)/shard_map/reduce_scatter | solution.py:73
  112.6 0.0 copy-start.3
  112.6 1.5 collective-permute-start.4
  114.0 29.2 %reduce-scatter.7.cloned.1.call-done = bf16[320,640]{1,0:T(8,128)(2,1)} async-done(((bf16[1280,640]{1,0:T(8,128)(2,1)}), bf16[320,640]{1,0:T(8,128)(2,1)}) %reduce-scatter.7.cloned.1.call-update) | async-done | bytes 409616
  143.3 1.3 copy.12
  144.5 1.0 copy.10
  145.5 0.2 broadcast_in_dim.9
  145.7 0.0 copy-done.3
  145.7 0.1 convert_dynamic-update-slice_fusion.1
  145.8 0.0 collective-permute-done.4
  145.8 0.1 convert_dynamic-update-slice_fusion
  145.9 0.0 copy-start.1
  146.0 1.4 copy-done.1
  (2 shorter events, 0.0 us)
Async XLA Ops:
  7.9 11.4 %collective-permute-start = (bf16[2,1280]{1,0:T(2,128)(2,1)S(1)}, bf16[2,1280]{1,0:T(2,128)(2,1)S(1)}, u32[]{:S(2)}, u32[]{:S(2)}) collective-permute-start(bf16[2,1280]{1,0:T(2,128)(2,1)S(1)} %get-tuple-element.15), channel_id=1, source_target_pairs={{0,4},{4,8},{8,12},{1,5},{5,9},{9,13},{2,6},{6,10},{10,14},{3,7},{... | collective-permute-start | bytes 15368 | tf_op jit(solution)/shard_map/ppermute | solution.py:11
  12.9 6.5 %collective-permute-start.1 = (bf16[2,1280]{1,0:T(2,128)(2,1)S(1)}, bf16[2,1280]{1,0:T(2,128)(2,1)S(1)}, u32[]{:S(2)}, u32[]{:S(2)}) collective-permute-start(bf16[2,1280]{1,0:T(2,128)(2,1)S(1)} %get-tuple-element.16), channel_id=1, source_target_pairs={{4,0},{8,4},{12,8},{5,1},{9,5},{13,9},{6,2},{10,6},{14,10},{7,3},{... | collective-permute-start | bytes 15368 | tf_op jit(solution)/shard_map/ppermute | solution.py:12
  15.9 16.0 %all-to-all-start = ((bf16[4,80,384]{2,1,0:T(8,128)(2,1)}), bf16[4,80,384]{2,1,0:T(8,128)(2,1)S(1)}, u32[]{:S(2)}, u32[]{:S(2)}) async-start(bf16[4,80,384]{2,1,0:T(8,128)(2,1)} %copy.9), calls=%async_computation | async-start | bytes 491520 | tf_op jit(solution)/shard_map/all_to_all | solution.py:35
  19.3 93.3 %reduce-scatter.5.cloned.1.call-start = ((), (), s32[]{:S(2)}) async-start(), calls=%async_computation.3 | async-start | bytes 3072000 | tf_op jit(solution)/shard_map/reduce_scatter | solution.py:73
  19.4 4.5 %copy-start.2 = (bf16[1,640,1280]{2,1,0:T(8,128)(2,1)S(1)}, bf16[1,640,1280]{2,1,0:T(8,128)(2,1)}, u32[]{:S(2)}) copy-start(bf16[1,640,1280]{2,1,0:T(8,128)(2,1)} %param.3) | copy-start | bytes 4915204
  22.3 21.5 %collective-permute-start.3 = (bf16[644,640]{1,0:T(8,128)(2,1)}, bf16[644,640]{1,0:T(8,128)(2,1)S(1)}, u32[]{:S(2)}, u32[]{:S(2)}) collective-permute-start(bf16[644,640]{1,0:T(8,128)(2,1)} %constant_dynamic-slice_fusion.1), channel_id=1, source_target_pairs={{0,16},{16,0},{1,17},{17,1},{2,18},{18,2},{3,19},{19,3},{4,20},{20... | collective-permute-start | bytes 2472968 | tf_op jit(solution)/shard_map/ppermute | solution.py:47
  39.6 14.2 %collective-permute-start.2 = (bf16[640,384]{1,0:T(8,128)(2,1)S(1)}, bf16[640,384]{1,0:T(8,128)(2,1)S(1)}, u32[]{:S(2)}, u32[]{:S(2)}) collective-permute-start(bf16[640,384]{1,0:T(8,128)(2,1)S(1)} %fusion.71), channel_id=1, source_target_pairs={{0,16},{16,0},{1,17},{17,1},{2,18},{18,2},{3,19},{19,3},{4,20},{20... | collective-permute-start | bytes 1474568 | tf_op jit(solution)/shard_map/ppermute | solution.py:60
  58.9 1.4 copy-start
  60.4 82.9 %reduce-scatter.7.cloned.1.call-start = ((), (), s32[]{:S(2)}) async-start(), calls=%async_computation.4 | async-start | bytes 2048000
  60.4 6.7 %collective-permute-start.5 = (bf16[2,384]{1,0:T(2,128)(2,1)S(1)}, bf16[2,384]{1,0:T(2,128)(2,1)S(1)}, u32[]{:S(2)}, u32[]{:S(2)}) collective-permute-start(bf16[2,384]{1,0:T(2,128)(2,1)S(1)} %get-tuple-element.23), channel_id=1, source_target_pairs={{4,0},{8,4},{12,8},{5,1},{9,5},{13,9},{6,2},{10,6},{14,10},{7,3},{... | collective-permute-start | bytes 4616 | tf_op jit(solution)/shard_map/ppermute | solution.py:12
  61.7 6.5 %collective-permute-start.6 = (bf16[2,384]{1,0:T(2,128)(2,1)S(1)}, bf16[2,384]{1,0:T(2,128)(2,1)S(1)}, u32[]{:S(2)}, u32[]{:S(2)}) collective-permute-start(bf16[2,384]{1,0:T(2,128)(2,1)S(1)} %get-tuple-element.22), channel_id=1, source_target_pairs={{0,4},{4,8},{8,12},{1,5},{5,9},{9,13},{2,6},{6,10},{10,14},{3,7},{... | collective-permute-start | bytes 4616 | tf_op jit(solution)/shard_map/ppermute | solution.py:11
  112.6 33.1 %copy-start.3 = (bf16[96,5,640]{2,0,1:T(8,128)(2,1)S(1)}, bf16[96,5,640]{2,0,1:T(8,128)(2,1)}, u32[]{:S(2)}) copy-start(bf16[96,5,640]{2,0,1:T(8,128)(2,1)} %reduce-scatter.5.cloned.1.call-done) | copy-start | bytes 1843204
  112.6 33.3 %collective-permute-start.4 = (bf16[96,5,640]{2,0,1:T(8,128)(2,1)}, bf16[96,5,640]{2,0,1:T(8,128)(2,1)S(1)}, u32[]{:S(2)}, u32[]{:S(2)}) collective-permute-start(bf16[96,5,640]{2,0,1:T(8,128)(2,1)} %reduce-scatter.5.cloned.1.call-done), channel_id=1, source_target_pairs={{0,16},{16,0},{1,17},{17,1},{2,18},{18,2},{3,19},{19,3},{4,20},{20... | collective-permute-start | bytes 1843208 | tf_op jit(solution)/shard_map/ppermute | solution.py:88
  145.9 1.4 copy-start.1
Sparse Core Ops, SparseCore 0:
  60.5 52.0 reduce-scatter.4
  115.1 28.1 reduce-scatter.6

commit v2 on v1

--- a/solution.py
+++ b/solution.py
@@ -1,6 +1,10 @@
+import functools
+
 import jax
 import jax.numpy as jnp
 from jax import lax
+from jax.experimental import pallas as pl
+from jax.experimental.pallas import tpu as pltpu
 from jax.sharding import PartitionSpec as P
 
 
@@ -92,9 +96,474 @@
     return (weight_grad, input_rows[None])
 
 
+MESH = pl.DeviceIdType.MESH
+EDGE = 16
+
+
+def fused_kernel(
+    n_seq,
+    n_section,
+    signal,
+    flat_hbm,
+    trunk,
+    weight_out,
+    input_out,
+    ext,
+    flat,
+    pooled,
+    prod,
+    linear,
+    grad_b,
+    grad_f,
+    grad_halo,
+    stacked,
+    grad_t,
+    other,
+    shift,
+    windows,
+    input_part,
+    input_recv,
+    weight_f,
+    ring_send,
+    ring_up,
+    ring_down,
+    last_send,
+    last_recv,
+    load_sem,
+    halo_sem,
+    trunk_sem,
+    signal_sem,
+    grad_sem,
+    input_sem,
+    ring_send_sem,
+    ring_up_sem,
+    ring_down_sem,
+    last_sem,
+):
+    f32, bf16 = jnp.float32, jnp.bfloat16
+    d, z, s = lax.axis_index("dp"), lax.axis_index("seq"), lax.axis_index("section")
+    length, c_in = signal.shape
+    c_out = pooled.shape[1]
+    rows = trunk.shape[0]
+    taps = flat.shape[0] // c_out
+    half = c_in // 2
+    part = length // 2
+    width = taps // 2
+    share = c_out // n_seq
+    block = c_in // n_section
+    end = EDGE + length
+    core = lax.rem(s, 2)
+    sibling = s + 1 - 2 * core
+    last = n_seq - 1
+
+    def to_dp():
+        return {"dp": 1 - d}
+
+    def to_seq(target):
+        return {"seq": target}
+
+    def to_section(target):
+        return {"section": target}
+
+    def remote(src, dst, send, recv, target):
+        return pltpu.make_async_remote_copy(
+            src_ref=src,
+            dst_ref=dst,
+            send_sem=send,
+            recv_sem=recv,
+            device_id=target,
+            device_id_type=MESH,
+        )
+
+    mine = pl.ds(pl.multiple_of(d * half, 128), half)
+    theirs = pl.ds(pl.multiple_of((1 - d) * half, 128), half)
+    own_rows = pl.ds(pl.multiple_of(s * rows, EDGE), rows)
+
+    load_signal = pltpu.make_async_copy(signal, ext.at[EDGE:end], load_sem.at[0])
+    load_flat = pltpu.make_async_copy(flat_hbm, flat, load_sem.at[1])
+    load_trunk = pltpu.make_async_copy(
+        trunk.at[:, pl.ds(pl.multiple_of(s * c_out, 128), c_out)], pooled.at[own_rows], load_sem.at[2]
+    )
+    load_signal.start()
+    load_flat.start()
+    load_trunk.start()
+
+    @pl.when(z == 0)
+    def _():
+        ext[0:EDGE] = jnp.zeros((EDGE, c_in), bf16)
+        grad_halo[0] = jnp.zeros((EDGE, c_out), bf16)
+
+    @pl.when(z == last)
+    def _():
+        ext[end : end + EDGE] = jnp.zeros((EDGE, c_in), bf16)
+        grad_halo[1] = jnp.zeros((EDGE, c_out), bf16)
+
+    barrier = pltpu.get_barrier_semaphore()
+    pl.semaphore_signal(barrier, inc=1, device_id=to_dp(), device_id_type=MESH)
+    for step in range(1, n_section):
+        pl.semaphore_signal(
+            barrier, inc=1, device_id=to_section(lax.rem(s + step, n_section)), device_id_type=MESH
+        )
+
+    @pl.when(z > 0)
+    def _():
+        pl.semaphore_signal(barrier, inc=1, device_id=to_seq(z - 1), device_id_type=MESH)
+
+    @pl.when(z < last)
+    def _():
+        pl.semaphore_signal(barrier, inc=1, device_id=to_seq(z + 1), device_id_type=MESH)
+
+    @pl.when(jnp.logical_and(z > 0, z < last))
+    def _():
+        pl.semaphore_wait(barrier, n_section + 2)
+
+    @pl.when(jnp.logical_or(z == 0, z == last))
+    def _():
+        pl.semaphore_wait(barrier, n_section + 1)
+
+    signal_up = remote(
+        signal.at[length - EDGE : length], ext.at[0:EDGE], halo_sem.at[0], halo_sem.at[1], to_seq(z + 1)
+    )
+    signal_down = remote(
+        signal.at[0:EDGE], ext.at[end : end + EDGE], halo_sem.at[2], halo_sem.at[3], to_seq(z - 1)
+    )
+
+    @pl.when(z < last)
+    def _():
+        signal_up.start()
+
+    @pl.when(z > 0)
+    def _():
+        signal_down.start()
+
+    trunk_copies = []
+    for step in range(1, n_section):
+        target = lax.rem(s + step, n_section)
+        copy = remote(
+            trunk.at[:, pl.ds(pl.multiple_of(target * c_out, 128), c_out)],
+            pooled.at[own_rows],
+            trunk_sem.at[0, step - 1],
+            trunk_sem.at[1, step - 1],
+            to_section(target),
+        )
+        copy.start()
+        trunk_copies.append(copy)
+
+    signal_cross = remote(
+        signal.at[pl.ds(pl.multiple_of(core * part, EDGE), part), theirs],
+        other.at[pl.ds(pl.multiple_of(EDGE + core * part, EDGE), part)],
+        signal_sem.at[0],
+        signal_sem.at[1],
+        to_dp(),
+    )
+    signal_cross.start()
+    brought = other.at[pl.ds(pl.multiple_of(EDGE + core * part, EDGE), part)]
+    signal_pass = remote(brought, brought, signal_sem.at[2], signal_sem.at[3], to_section(sibling))
+    edge_low = remote(
+        ext.at[0:EDGE, theirs], other.at[0:EDGE], signal_sem.at[4], signal_sem.at[5], to_dp()
+    )
+    edge_high = remote(
+        ext.at[end : end + EDGE, theirs],
+        other.at[end : end + EDGE],
+        signal_sem.at[6],
+        signal_sem.at[7],
+        to_dp(),
+    )
+
+    load_signal.wait()
+
+    @pl.when(z < last)
+    def _():
+        signal_up.wait_send()
+        signal_down.wait_recv()
+
+    @pl.when(z > 0)
+    def _():
+        signal_down.wait_send()
+        signal_up.wait_recv()
+
+    edge_low.start()
+    edge_high.start()
+    load_flat.wait()
+
+    for tap in range(taps):
+        prod[...] = lax.dot_general(
+            ext[...],
+            flat[tap * c_out : (tap + 1) * c_out],
+            (((1,), (1,)), ((), ())),
+            preferred_element_type=f32,
+        )
+        moved = prod[EDGE - width + tap : EDGE - width + tap + length]
+        if tap == 0:
+            linear[...] = moved
+        else:
+            linear[...] += moved
+
+    load_trunk.wait()
+    for copy in trunk_copies:
+        copy.wait()
+
+    doubled = jnp.where(
+        lax.broadcasted_iota(jnp.int32, (length, length // 2), 0) // 2
+        == lax.broadcasted_iota(jnp.int32, (length, length // 2), 1),
+        0.5,
+        0.0,
+    ).astype(bf16)
+    grad_f[EDGE:end] = lax.dot_general(
+        doubled, pooled[...], (((1,), (0,)), ((), ())), preferred_element_type=f32
+    )
+    values = linear[...]
+    normal_cdf = 0.5 * (1.0 + lax.erf(values * 0.7071067811865476))
+    density = jnp.exp(-0.5 * values * values) * 0.3989422804014327
+    grad_b[...] = (grad_f[EDGE:end] * (normal_cdf + values * density)).astype(bf16)
+
+    grad_up = remote(
+        grad_b.at[length - EDGE : length], grad_halo.at[0], grad_sem.at[0], grad_sem.at[1], to_seq(z + 1)
+    )
+    grad_down = remote(
+        grad_b.at[0:EDGE], grad_halo.at[1], grad_sem.at[2], grad_sem.at[3], to_seq(z - 1)
+    )
+
+    @pl.when(z < last)
+    def _():
+        grad_up.start()
+
+    @pl.when(z > 0)
+    def _():
+        grad_down.start()
+
+    grad_f[EDGE:end] = grad_b[...].astype(f32)
+    grad_t[0] = grad_f[EDGE:end].T.astype(bf16)
+    grad_cross = remote(grad_t.at[0], grad_t.at[1], grad_sem.at[4], grad_sem.at[5], to_dp())
+    grad_cross.start()
+
+    signal_cross.wait_recv()
+    signal_pass.start()
+
+    @pl.when(z < last)
+    def _():
+        grad_up.wait_send()
+        grad_down.wait_recv()
+
+    @pl.when(z > 0)
+    def _():
+        grad_down.wait_send()
+        grad_up.wait_recv()
+
+    grad_f[0:EDGE] = grad_halo[0].astype(f32)
+    grad_f[end : end + EDGE] = grad_halo[1].astype(f32)
+    for tap in range(taps):
+        begin = EDGE + width - tap
+        stacked[:, tap * c_out : (tap + 1) * c_out] = grad_f[begin : begin + length].astype(bf16)
+    for column in range(0, c_in, 256):
+        piece = lax.dot_general(
+            stacked[...],
+            flat[:, column : column + 256],
+            (((1,), (0,)), ((), ())),
+            preferred_element_type=f32,
+        )
+        input_part[column : column + 256] = piece.T.astype(bf16)
+    input_copies = []
+    for step in range(1, n_section):
+        target = lax.rem(s + step, n_section)
+        copy = remote(
+            input_part.at[pl.ds(pl.multiple_of(target * block, EDGE), block)],
+            input_recv.at[step - 1],
+            input_sem.at[0, step - 1],
+            input_sem.at[1, step - 1],
+            to_section(target),
+        )
+        copy.start()
+        input_copies.append(copy)
+
+    shift[...] = ext[:, mine].astype(f32)
+    for tap in range(taps):
+        begin = EDGE - width + tap
+        windows[0, tap] = shift[begin : begin + length].astype(bf16)
+    signal_cross.wait_send()
+    signal_pass.wait()
+    edge_low.wait()
+    edge_high.wait()
+    shift[...] = other[...].astype(f32)
+    for tap in range(taps):
+        begin = EDGE - width + tap
+        windows[1, tap] = shift[begin : begin + length].astype(bf16)
+    grad_cross.wait()
+
+    def up(tap, owner):
+        return remote(
+            ring_send.at[tap, owner],
+            ring_up.at[tap, owner],
+            ring_send_sem.at[tap, owner],
+            ring_up_sem.at[tap, owner],
+            to_seq(z + 1),
+        )
+
+    def down(tap, owner):
+        return remote(
+            ring_send.at[tap, owner],
+            ring_down.at[tap, owner],
+            ring_send_sem.at[tap, owner],
+            ring_down_sem.at[tap, owner],
+            to_seq(z - 1),
+        )
+
+    def own(tap, owner):
+        return weight_f[tap, owner * share : (owner + 1) * share]
+
+    for tap in range(taps):
+        weight_f[tap] = jnp.dot(
+            grad_t[0], windows[0, tap], preferred_element_type=f32
+        ) + jnp.dot(grad_t[1], windows[1, tap], preferred_element_type=f32)
+
+        @pl.when(z == 0)
+        def _():
+            for owner in range(last, 0, -1):
+                ring_send[tap, owner] = own(tap, owner).astype(bf16)
+                up(tap, owner).start()
+
+        @pl.when(z == last)
+        def _():
+            for owner in range(0, last):
+                ring_send[tap, owner] = own(tap, owner).astype(bf16)
+                down(tap, owner).start()
+
+    def finish(tap, total):
+        weight_out[tap, :, mine] = total
+        last_send[tap] = total.astype(bf16)
+
+    def cross(tap):
+        return remote(
+            last_send.at[tap], last_recv.at[tap], last_sem.at[0, tap], last_sem.at[1, tap], to_dp()
+        )
+
+    def relay_up(tap, owner):
+        up(tap, owner).wait_recv()
+        ring_send[tap, owner] = (own(tap, owner) + ring_up[tap, owner].astype(f32)).astype(bf16)
+        up(tap, owner).start()
+
+    def relay_down(tap, owner):
+        down(tap, owner).wait_recv()
+        ring_send[tap, owner] = (own(tap, owner) + ring_down[tap, owner].astype(f32)).astype(bf16)
+        down(tap, owner).start()
+
+    for tap in range(taps):
+        for place in range(n_seq):
+
+            @pl.when(z == place)
+            def _():
+                if 0 < place < last:
+                    ups = [(relay_up, owner) for owner in range(last, place, -1)]
+                    downs = [(relay_down, owner) for owner in range(0, place)]
+                    order = ups + downs if place < n_seq // 2 else downs + ups
+                    for relay, owner in order:
+                        relay(tap, owner)
+                total = own(tap, place)
+                if place > 0:
+                    up(tap, place).wait_recv()
+                    total = total + ring_up[tap, place].astype(f32)
+                if place < last:
+                    down(tap, place).wait_recv()
+                    total = total + ring_down[tap, place].astype(f32)
+                finish(tap, total)
+
+        cross(tap).start()
+
+        if tap == 0:
+            for copy in input_copies:
+                copy.wait()
+            summed = input_part[pl.ds(pl.multiple_of(s * block, EDGE), block)].astype(f32)
+            for step in range(1, n_section):
+                summed = summed + input_recv[step - 1].astype(f32)
+            input_out[...] = summed.astype(bf16)
+
+    for tap in range(taps):
+        cross(tap).wait()
+        weight_out[tap, :, theirs] = last_recv[tap].astype(f32)
+        for place in range(n_seq):
+
+            @pl.when(z == place)
+            def _():
+                for owner in range(n_seq):
+                    if owner > place:
+                        up(tap, owner).wait_send()
+                    elif owner < place:
+                        down(tap, owner).wait_send()
+
+
+def fused_shards(n_seq, n_section, signal, kernel, trunk_grad):
+    f32, bf16 = jnp.float32, jnp.bfloat16
+    _, length, c_in = signal.shape
+    c_out, taps, _ = kernel.shape
+    share, block, half = c_out // n_seq, c_in // n_section, c_in // 2
+    padded = length + 2 * EDGE
+    flat = jnp.transpose(kernel, (1, 0, 2)).reshape(taps * c_out, c_in)
+    vmem = pl.BlockSpec(memory_space=pltpu.VMEM)
+    hbm = pl.BlockSpec(memory_space=pl.ANY)
+    dma = pltpu.SemaphoreType.DMA
+    weight, rows = pl.pallas_call(
+        functools.partial(fused_kernel, n_seq, n_section),
+        out_shape=(
+            jax.ShapeDtypeStruct((taps, share, c_in), f32),
+            jax.ShapeDtypeStruct((block, length), bf16),
+        ),
+        in_specs=[hbm, hbm, hbm],
+        out_specs=(vmem, vmem),
+        scratch_shapes=[
+            pltpu.VMEM((padded, c_in), bf16),
+            pltpu.VMEM((taps * c_out, c_in), bf16),
+            pltpu.VMEM((length // 2, c_out), bf16),
+            pltpu.VMEM((padded, c_out), f32),
+            pltpu.VMEM((length, c_out), f32),
+            pltpu.VMEM((length, c_out), bf16),
+            pltpu.VMEM((padded, c_out), f32),
+            pltpu.VMEM((2, EDGE, c_out), bf16),
+            pltpu.VMEM((length, taps * c_out), bf16),
+            pltpu.VMEM((2, c_out, length), bf16),
+            pltpu.VMEM((padded, half), bf16),
+            pltpu.VMEM((padded, half), f32),
+            pltpu.VMEM((2, taps, length, half), bf16),
+            pltpu.VMEM((c_in, length), bf16),
+            pltpu.VMEM((n_section - 1, block, length), bf16),
+            pltpu.VMEM((taps, c_out, half), f32),
+            pltpu.VMEM((taps, n_seq, share, half), bf16),
+            pltpu.VMEM((taps, n_seq, share, half), bf16),
+            pltpu.VMEM((taps, n_seq, share, half), bf16),
+            pltpu.VMEM((taps, share, half), bf16),
+            pltpu.VMEM((taps, share, half), bf16),
+            dma((3,)),
+            dma((4,)),
+            dma((2, n_section - 1)),
+            dma((8,)),
+            dma((6,)),
+            dma((2, n_section - 1)),
+            dma((taps, n_seq)),
+            dma((taps, n_seq)),
+            dma((taps, n_seq)),
+            dma((2, taps)),
+        ],
+        compiler_params=pltpu.CompilerParams(
+            collective_id=0, has_side_effects=True, vmem_limit_bytes=60 * 1024 * 1024
+        ),
+        cost_estimate=pl.CostEstimate(
+            flops=6 * length * c_in * c_out * taps,
+            bytes_accessed=2 * (length * c_in + 3 * c_out * taps * c_in),
+            transcendentals=2 * length * c_out,
+        ),
+    )(signal[0], flat, trunk_grad[0])
+    return jnp.transpose(weight, (1, 0, 2)), rows[None]
+
+
+def fits(mesh):
+    return (mesh.shape["dp"], mesh.shape["seq"], mesh.shape["section"]) == (2, 4, 4)
+
+
 def solution(mesh):
+    body = shards
+    if fits(mesh):
+        body = functools.partial(fused_shards, mesh.shape["seq"], mesh.shape["section"])
     return jax.shard_map(
-        shards,
+        body,
         mesh=mesh,
         in_specs=(
             P("dp", "seq", None),

time: 155 us -> 85.9 us (0.55)
  Pallas kernels: 0 us -> 81 us
  waiting for transfers between devices: 76.8 us -> 0 us
  starting transfers between devices: 19.9 us -> 0 us
  matrix products: 19.3 us -> 0 us
  between operations: 14.3 us -> 0.65 us
  local copies, waits for them, and re-layouts: 17.6 us -> 4.16 us
  other arithmetic: 6.29 us -> 0 us
    pallas_call x0 -> x1, Pallas kernels: none -> 81 us  [fused_shards(): pl.pallas_call(functools.partial(fused_kernel, n_seq, n_section), out_sha...]
    reduce_scatter x1 -> x0, waiting for transfers between devices: 35.6 us -> none  [shards(): lax.psum_scatter(partial, 'seq', scatter_dimension=0, tiled=True)]
    unnamed x3 -> x0, waiting for transfers between devices: 29.3 us -> none
    dot_general x7 -> x0, matrix products: 19.3 us -> none  [the longest x1 8.04 us: shards(): lax.dot_general(padded, flat, (((1,), (1,)), ((), ())), preferred_element...]
    ppermute x7 -> x0, starting transfers between devices: 16.5 us -> none  [the longest x2 10.3 us: edges(): low = lax.ppermute(block[-width:], axis, forward)]
    ppermute x7 -> x0, waiting for transfers between devices: 11.9 us -> none  [the longest x1 9.28 us: shards(): grads.append(lax.ppermute(grad_pre, 'dp', rings[step]))]
    convert_element_type x1 -> x0, other arithmetic: 3.51 us -> none  [shards(): grad_pre = (grad_hidden * gelu_slope(linear)).astype(jnp.bfloat16)]
    all_to_all x1 -> x0, starting transfers between devices: 3.4 us -> none  [shards(): lax.all_to_all(trunk, 'section', split_axis=0, concat_axis=0)]
  transfers between devices with their start and end apart: 10 -> 0, of which waited for: 5 -> 0; matrix products, arithmetic and copies ran while one was open for 22% -> 0% of each run, Pallas kernels for 0% -> 0%
where the time goes in v2:
time: 85.9 us; the launch traced here: 85.8 us
  Pallas kernels  81 us (94%)
  local copies, waits for them, and re-layouts  4.16 us (5%)
    pallas_call x1, Pallas kernels, fused_shards(): pl.pallas_call(functools.partial(fused_kernel, n_seq, n_section), out_sha...  81 us
    unnamed x4, local copies, waits for them, and re-layouts  4.16 us

profile of v2, /device:TPU:0, one launch (start us, length us, event | category | flops | bytes accessed | tf_op | source)
XLA Modules:
  0.0 85.8 jit_solution(16673539905567637819)
XLA Ops:
  0.6 81.0 %shard_map.50 = (f32[5,96,1280]{2,1,0:T(8,128)}, bf16[320,640]{1,0:T(8,128)(2,1)}) custom-call(bf16[640,1280]{1,0:T(8,128)(2,1)} %bitcast.10, bf16[1920,1280]{1,0:T(8,128)(2,1)} %bitcast.9, bf16[80,1536]{1,0:T(8,128)(2,1)} %bitcast.11), custom_call_target="tpu_custom_call" | custom-call | flops 9437184000 | bytes 16384000 | tf_op jit(solution)/shard_map/pallas_call | solution.py:504
  81.6 0.0 copy-start
  81.6 3.4 %copy.7 = f32[96,5,1280]{2,0,1:T(8,128)} copy(f32[96,5,1280]{2,0,1:T(8,128)} %bitcast.7) | data formatting | bytes 4915200
  85.0 0.0 copy-done
  85.0 0.8 copy.8
Async XLA Ops:
  81.6 3.4 %copy-start = (bf16[320,640]{1,0:T(8,128)(2,1)S(1)}, bf16[320,640]{1,0:T(8,128)(2,1)}, u32[]{:S(2)}) copy-start(bf16[320,640]{1,0:T(8,128)(2,1)} %get-tuple-element.5) | copy-start | bytes 1228804

commit v3 on v2

--- a/solution.py
+++ b/solution.py
@@ -127,8 +127,6 @@
     ring_send,
     ring_up,
     ring_down,
-    last_send,
-    last_recv,
     load_sem,
     halo_sem,
     trunk_sem,
@@ -150,6 +148,7 @@
     part = length // 2
     width = taps // 2
     share = c_out // n_seq
+    band = c_out // 2
     block = c_in // n_section
     end = EDGE + length
     core = lax.rem(s, 2)
@@ -334,61 +333,29 @@
 
     grad_f[EDGE:end] = grad_b[...].astype(f32)
     grad_t[0] = grad_f[EDGE:end].T.astype(bf16)
-    grad_cross = remote(grad_t.at[0], grad_t.at[1], grad_sem.at[4], grad_sem.at[5], to_dp())
-    grad_cross.start()
+    first = jnp.where(z < n_seq // 2, 1, 0)
+    bands = [pl.ds(pl.multiple_of(at * band, EDGE), band) for at in (first, 1 - first)]
+    grad_crosses = []
+    for at in range(2):
+        copy = remote(
+            grad_t.at[0, bands[at]],
+            grad_t.at[1, bands[at]],
+            grad_sem.at[4 + 2 * at],
+            grad_sem.at[5 + 2 * at],
+            to_dp(),
+        )
+        copy.start()
+        grad_crosses.append(copy)
 
     signal_cross.wait_recv()
     signal_pass.start()
 
-    @pl.when(z < last)
-    def _():
-        grad_up.wait_send()
-        grad_down.wait_recv()
-
-    @pl.when(z > 0)
-    def _():
-        grad_down.wait_send()
-        grad_up.wait_recv()
-
-    grad_f[0:EDGE] = grad_halo[0].astype(f32)
-    grad_f[end : end + EDGE] = grad_halo[1].astype(f32)
-    for tap in range(taps):
-        begin = EDGE + width - tap
-        stacked[:, tap * c_out : (tap + 1) * c_out] = grad_f[begin : begin + length].astype(bf16)
-    for column in range(0, c_in, 256):
-        piece = lax.dot_general(
-            stacked[...],
-            flat[:, column : column + 256],
-            (((1,), (0,)), ((), ())),
-            preferred_element_type=f32,
-        )
-        input_part[column : column + 256] = piece.T.astype(bf16)
-    input_copies = []
-    for step in range(1, n_section):
-        target = lax.rem(s + step, n_section)
-        copy = remote(
-            input_part.at[pl.ds(pl.multiple_of(target * block, EDGE), block)],
-            input_recv.at[step - 1],
-            input_sem.at[0, step - 1],
-            input_sem.at[1, step - 1],
-            to_section(target),
-        )
-        copy.start()
-        input_copies.append(copy)
-
-    shift[...] = ext[:, mine].astype(f32)
-    for tap in range(taps):
-        begin = EDGE - width + tap
-        windows[0, tap] = shift[begin : begin + length].astype(bf16)
+    shift[0] = ext[:, mine].astype(f32)
     signal_cross.wait_send()
     signal_pass.wait()
     edge_low.wait()
     edge_high.wait()
-    shift[...] = other[...].astype(f32)
-    for tap in range(taps):
-        begin = EDGE - width + tap
-        windows[1, tap] = shift[begin : begin + length].astype(bf16)
-    grad_cross.wait()
+    shift[1] = other[...].astype(f32)
 
     def up(tap, owner):
         return remote(
@@ -411,30 +378,12 @@
     def own(tap, owner):
         return weight_f[tap, owner * share : (owner + 1) * share]
 
-    for tap in range(taps):
-        weight_f[tap] = jnp.dot(
-            grad_t[0], windows[0, tap], preferred_element_type=f32
-        ) + jnp.dot(grad_t[1], windows[1, tap], preferred_element_type=f32)
-
-        @pl.when(z == 0)
-        def _():
-            for owner in range(last, 0, -1):
-                ring_send[tap, owner] = own(tap, owner).astype(bf16)
-                up(tap, owner).start()
-
-        @pl.when(z == last)
-        def _():
-            for owner in range(0, last):
-                ring_send[tap, owner] = own(tap, owner).astype(bf16)
-                down(tap, owner).start()
-
     def finish(tap, total):
-        weight_out[tap, :, mine] = total
-        last_send[tap] = total.astype(bf16)
+        weight_out[tap, :, mine] = total.astype(bf16)
 
     def cross(tap):
         return remote(
-            last_send.at[tap], last_recv.at[tap], last_sem.at[0, tap], last_sem.at[1, tap], to_dp()
+            weight_out.at[tap, :, mine], weight_out.at[tap, :, mine], last_sem.at[0, tap], last_sem.at[1, tap], to_dp()
         )
 
     def relay_up(tap, owner):
@@ -447,17 +396,117 @@
         ring_send[tap, owner] = (own(tap, owner) + ring_down[tap, owner].astype(f32)).astype(bf16)
         down(tap, owner).start()
 
+    def multiply(tap, at):
+        weight_f[tap, bands[at]] = jnp.dot(
+            grad_t[0, bands[at]], windows[0, tap], preferred_element_type=f32
+        ) + jnp.dot(grad_t[1, bands[at]], windows[1, tap], preferred_element_type=f32)
+
+    def send_up(tap, owners):
+        for owner in owners:
+            ring_send[tap, owner] = own(tap, owner).astype(bf16)
+            up(tap, owner).start()
+
+    def send_down(tap, owners):
+        for owner in owners:
+            ring_send[tap, owner] = own(tap, owner).astype(bf16)
+            down(tap, owner).start()
+
+    def relay(tap, place, band_at):
+        low_band = range(0, n_seq // 2)
+        owners = low_band if (place >= n_seq // 2) == (band_at == 0) else range(n_seq // 2, n_seq)
+        for owner in reversed(owners):
+            if owner > place:
+                relay_up(tap, owner)
+        for owner in owners:
+            if owner < place:
+                relay_down(tap, owner)
+
+    middle = n_seq // 2
+    for tap in range(taps):
+        begin = EDGE - width + tap
+        for source in range(2):
+            windows[source, tap] = shift[source, begin : begin + length].astype(bf16)
+        if tap == 0:
+            grad_crosses[0].wait()
+        multiply(tap, 0)
+
+        @pl.when(z == 0)
+        def _():
+            send_up(tap, range(last, middle - 1, -1))
+
+        @pl.when(z == last)
+        def _():
+            send_down(tap, range(0, middle))
+
+    @pl.when(z < last)
+    def _():
+        grad_up.wait_send()
+        grad_down.wait_recv()
+
+    @pl.when(z > 0)
+    def _():
+        grad_down.wait_send()
+        grad_up.wait_recv()
+
+    grad_f[0:EDGE] = grad_halo[0].astype(f32)
+    grad_f[end : end + EDGE] = grad_halo[1].astype(f32)
+    for tap in range(taps):
+        begin = EDGE + width - tap
+        stacked[:, tap * c_out : (tap + 1) * c_out] = grad_f[begin : begin + length].astype(bf16)
+
+    def input_columns(column):
+        piece = lax.dot_general(
+            stacked[...],
+            flat[:, column : column + 256],
+            (((1,), (0,)), ((), ())),
+            preferred_element_type=f32,
+        )
+        input_part[column : column + 256] = piece.T.astype(bf16)
+
+    input_copies = []
+    pending = list(range(0, c_in, 256))
+    grad_crosses[1].wait()
+    for tap in range(taps):
+        multiply(tap, 1)
+
+        @pl.when(z == 0)
+        def _():
+            send_up(tap, range(middle - 1, 0, -1))
+
+        @pl.when(z == last)
+        def _():
+            send_down(tap, range(middle, last))
+
+        if pending:
+            for column in pending[:2]:
+                input_columns(column)
+            pending = pending[2:]
+            if not pending:
+                for step in range(1, n_section):
+                    target = lax.rem(s + step, n_section)
+                    copy = remote(
+                        input_part.at[pl.ds(pl.multiple_of(target * block, EDGE), block)],
+                        input_recv.at[step - 1],
+                        input_sem.at[0, step - 1],
+                        input_sem.at[1, step - 1],
+                        to_section(target),
+                    )
+                    copy.start()
+                    input_copies.append(copy)
+
+        for place in range(1, last):
+
+            @pl.when(z == place)
+            def _():
+                relay(tap, place, 0)
+
     for tap in range(taps):
         for place in range(n_seq):
 
             @pl.when(z == place)
             def _():
                 if 0 < place < last:
-                    ups = [(relay_up, owner) for owner in range(last, place, -1)]
-                    downs = [(relay_down, owner) for owner in range(0, place)]
-                    order = ups + downs if place < n_seq // 2 else downs + ups
-                    for relay, owner in order:
-                        relay(tap, owner)
+                    relay(tap, place, 1)
                 total = own(tap, place)
                 if place > 0:
                     up(tap, place).wait_recv()
@@ -469,17 +518,15 @@
 
         cross(tap).start()
 
-        if tap == 0:
-            for copy in input_copies:
-                copy.wait()
-            summed = input_part[pl.ds(pl.multiple_of(s * block, EDGE), block)].astype(f32)
-            for step in range(1, n_section):
-                summed = summed + input_recv[step - 1].astype(f32)
-            input_out[...] = summed.astype(bf16)
+    for copy in input_copies:
+        copy.wait()
+    summed = input_part[pl.ds(pl.multiple_of(s * block, EDGE), block)].astype(f32)
+    for step in range(1, n_section):
+        summed = summed + input_recv[step - 1].astype(f32)
+    input_out[...] = summed.astype(bf16)
 
     for tap in range(taps):
         cross(tap).wait()
-        weight_out[tap, :, theirs] = last_recv[tap].astype(f32)
         for place in range(n_seq):
 
             @pl.when(z == place)
@@ -504,7 +551,7 @@
     weight, rows = pl.pallas_call(
         functools.partial(fused_kernel, n_seq, n_section),
         out_shape=(
-            jax.ShapeDtypeStruct((taps, share, c_in), f32),
+            jax.ShapeDtypeStruct((taps, share, c_in), bf16),
             jax.ShapeDtypeStruct((block, length), bf16),
         ),
         in_specs=[hbm, hbm, hbm],
@@ -521,7 +568,7 @@
             pltpu.VMEM((length, taps * c_out), bf16),
             pltpu.VMEM((2, c_out, length), bf16),
             pltpu.VMEM((padded, half), bf16),
-            pltpu.VMEM((padded, half), f32),
+            pltpu.VMEM((2, padded, half), f32),
             pltpu.VMEM((2, taps, length, half), bf16),
             pltpu.VMEM((c_in, length), bf16),
             pltpu.VMEM((n_section - 1, block, length), bf16),
@@ -529,13 +576,11 @@
             pltpu.VMEM((taps, n_seq, share, half), bf16),
             pltpu.VMEM((taps, n_seq, share, half), bf16),
             pltpu.VMEM((taps, n_seq, share, half), bf16),
-            pltpu.VMEM((taps, share, half), bf16),
-            pltpu.VMEM((taps, share, half), bf16),
             dma((3,)),
             dma((4,)),
             dma((2, n_section - 1)),
             dma((8,)),
-            dma((6,)),
+            dma((8,)),
             dma((2, n_section - 1)),
             dma((taps, n_seq)),
             dma((taps, n_seq)),
@@ -551,7 +596,7 @@
             transcendentals=2 * length * c_out,
         ),
     )(signal[0], flat, trunk_grad[0])
-    return jnp.transpose(weight, (1, 0, 2)), rows[None]
+    return jnp.transpose(weight.astype(f32), (1, 0, 2)), rows[None]
 
 
 def fits(mesh):

time: 85.9 us -> 75 us (0.87)
  Pallas kernels: 81 us -> 70.4 us
  local copies, waits for them, and re-layouts: 4.16 us -> 0.76 us
  other arithmetic: 0 us -> 2.98 us
    pallas_call x1, Pallas kernels: 81 us -> 70.4 us  [fused_shards(): pl.pallas_call(functools.partial(fused_kernel, n_seq, n_section), out_sha...]
    unnamed x4 -> x3, local copies, waits for them, and re-layouts: 4.16 us -> 0.76 us
    transpose x0 -> x1, other arithmetic: none -> 2.98 us  [fused_shards(): return (jnp.transpose(weight.astype(f32), (1, 0, 2)), rows[None])]
where the time goes in v3:
time: 75 us; the launch traced here: 74.8 us
  Pallas kernels  70.4 us (94%)
  other arithmetic  2.98 us (4%)
  local copies, waits for them, and re-layouts  0.76 us (1%)
    pallas_call x1, Pallas kernels, fused_shards(): pl.pallas_call(functools.partial(fused_kernel, n_seq, n_section), out_sha...  70.4 us
    transpose x1, other arithmetic, fused_shards(): return (jnp.transpose(weight.astype(f32), (1, 0, 2)), rows[None])  2.98 us

profile of v3, /device:TPU:0, one launch (start us, length us, event | category | flops | bytes accessed | tf_op | source)
XLA Modules:
  0.0 74.8 jit_solution(10861387912104182686)
XLA Ops:
  0.6 70.4 %shard_map.50 = (bf16[5,96,1280]{2,1,0:T(8,128)(2,1)}, bf16[320,640]{1,0:T(8,128)(2,1)}) custom-call(bf16[640,1280]{1,0:T(8,128)(2,1)} %bitcast.10, bf16[1920,1280]{1,0:T(8,128)(2,1)} %bitcast.9, bf16[80,1536]{1,0:T(8,128)(2,1)} %bitcast.11), custom_call_target="tpu_custom_call" | custom-call | flops 9437184000 | bytes 16384000 | tf_op jit(solution)/shard_map/pallas_call | solution.py:551
  71.1 0.0 copy-start
  71.1 3.0 %convert_bitcast_fusion = f32[96,5,1280]{2,0,1:T(8,128)} fusion(bf16[5,96,1280]{2,1,0:T(8,128)(2,1)} %get-tuple-element.4), kind=kLoop, calls=%fused_computation | loop fusion | flops 614400 | bytes 3686400 | tf_op jit(solution)/shard_map/transpose | solution.py:599
  74.1 0.0 copy-done
  74.1 0.8 %copy.6 = bf16[1,320,640]{2,1,0:T(8,128)(2,1)} copy(bf16[1,320,640]{2,1,0:T(8,128)(2,1)S(1)} %bitcast.8) | data formatting | bytes 819200
Async XLA Ops:
  71.1 3.0 %copy-start = (bf16[320,640]{1,0:T(8,128)(2,1)S(1)}, bf16[320,640]{1,0:T(8,128)(2,1)}, u32[]{:S(2)}) copy-start(bf16[320,640]{1,0:T(8,128)(2,1)} %get-tuple-element.5) | copy-start | bytes 1228804

commit v4 on v3

--- a/solution.py
+++ b/solution.py
@@ -285,58 +285,44 @@
     edge_high.start()
     load_flat.wait()
 
-    for tap in range(taps):
-        prod[...] = lax.dot_general(
-            ext[...],
-            flat[tap * c_out : (tap + 1) * c_out],
-            (((1,), (1,)), ((), ())),
-            preferred_element_type=f32,
-        )
-        moved = prod[EDGE - width + tap : EDGE - width + tap + length]
-        if tap == 0:
-            linear[...] = moved
-        else:
-            linear[...] += moved
-
-    load_trunk.wait()
-    for copy in trunk_copies:
-        copy.wait()
-
-    doubled = jnp.where(
-        lax.broadcasted_iota(jnp.int32, (length, length // 2), 0) // 2
-        == lax.broadcasted_iota(jnp.int32, (length, length // 2), 1),
-        0.5,
-        0.0,
-    ).astype(bf16)
-    grad_f[EDGE:end] = lax.dot_general(
-        doubled, pooled[...], (((1,), (0,)), ((), ())), preferred_element_type=f32
-    )
-    values = linear[...]
-    normal_cdf = 0.5 * (1.0 + lax.erf(values * 0.7071067811865476))
-    density = jnp.exp(-0.5 * values * values) * 0.3989422804014327
-    grad_b[...] = (grad_f[EDGE:end] * (normal_cdf + values * density)).astype(bf16)
-
-    grad_up = remote(
-        grad_b.at[length - EDGE : length], grad_halo.at[0], grad_sem.at[0], grad_sem.at[1], to_seq(z + 1)
-    )
-    grad_down = remote(
-        grad_b.at[0:EDGE], grad_halo.at[1], grad_sem.at[2], grad_sem.at[3], to_seq(z - 1)
-    )
-
-    @pl.when(z < last)
-    def _():
-        grad_up.start()
-
-    @pl.when(z > 0)
-    def _():
-        grad_down.start()
-
-    grad_f[EDGE:end] = grad_b[...].astype(f32)
-    grad_t[0] = grad_f[EDGE:end].T.astype(bf16)
     first = jnp.where(z < n_seq // 2, 1, 0)
-    bands = [pl.ds(pl.multiple_of(at * band, EDGE), band) for at in (first, 1 - first)]
+    halves = [first, 1 - first]
+    bands = [pl.ds(pl.multiple_of(at * band, EDGE), band) for at in halves]
     grad_crosses = []
     for at in range(2):
+        for tap in range(taps):
+            prod[:, 0:band] = lax.dot_general(
+                ext[...],
+                flat[pl.ds(pl.multiple_of(tap * c_out + halves[at] * band, EDGE), band)],
+                (((1,), (1,)), ((), ())),
+                preferred_element_type=f32,
+            )
+            moved = prod[EDGE - width + tap : EDGE - width + tap + length, 0:band]
+            if tap == 0:
+                linear[:, 0:band] = moved
+            else:
+                linear[:, 0:band] += moved
+        if at == 0:
+            load_trunk.wait()
+            for copy in trunk_copies:
+                copy.wait()
+            doubled = jnp.where(
+                lax.broadcasted_iota(jnp.int32, (length, length // 2), 0) // 2
+                == lax.broadcasted_iota(jnp.int32, (length, length // 2), 1),
+                0.5,
+                0.0,
+            ).astype(bf16)
+            grad_f[EDGE:end] = lax.dot_general(
+                doubled, pooled[...], (((1,), (0,)), ((), ())), preferred_element_type=f32
+            )
+        hidden = jnp.where(
+            halves[at] == 1, grad_f[EDGE:end, band : 2 * band], grad_f[EDGE:end, 0:band]
+        )
+        values = linear[:, 0:band]
+        normal_cdf = 0.5 * (1.0 + lax.erf(values * 0.7071067811865476))
+        density = jnp.exp(-0.5 * values * values) * 0.3989422804014327
+        banded = hidden * (normal_cdf + values * density)
+        grad_t[0, bands[at]] = banded.T.astype(bf16)
         copy = remote(
             grad_t.at[0, bands[at]],
             grad_t.at[1, bands[at]],
@@ -346,6 +332,24 @@
         )
         copy.start()
         grad_crosses.append(copy)
+
+    grad_f[EDGE:end] = grad_t[0].astype(f32).T
+    grad_b[...] = grad_f[EDGE:end].astype(bf16)
+
+    grad_up = remote(
+        grad_b.at[length - EDGE : length], grad_halo.at[0], grad_sem.at[0], grad_sem.at[1], to_seq(z + 1)
+    )
+    grad_down = remote(
+        grad_b.at[0:EDGE], grad_halo.at[1], grad_sem.at[2], grad_sem.at[3], to_seq(z - 1)
+    )
+
+    @pl.when(z < last)
+    def _():
+        grad_up.start()
+
+    @pl.when(z > 0)
+    def _():
+        grad_down.start()
 
     signal_cross.wait_recv()
     signal_pass.start()

time: 75 us -> 75.3 us (level)
  no operation moved by 1% of the time
where the time goes in v4:
time: 75.3 us; the launch traced here: 75.1 us
  Pallas kernels  70.7 us (94%)
  other arithmetic  2.98 us (4%)
  local copies, waits for them, and re-layouts  0.76 us (1%)
    pallas_call x1, Pallas kernels, fused_shards(): pl.pallas_call(functools.partial(fused_kernel, n_seq, n_section), out_sha...  70.7 us
    transpose x1, other arithmetic, fused_shards(): return (jnp.transpose(weight.astype(f32), (1, 0, 2)), rows[None])  2.98 us

profile of v4, /device:TPU:0, one launch (start us, length us, event | category | flops | bytes accessed | tf_op | source)
XLA Modules:
  0.0 75.1 jit_solution(9050501719985101892)
XLA Ops:
  0.6 70.7 %shard_map.50 = (bf16[5,96,1280]{2,1,0:T(8,128)(2,1)}, bf16[320,640]{1,0:T(8,128)(2,1)}) custom-call(bf16[640,1280]{1,0:T(8,128)(2,1)} %bitcast.10, bf16[1920,1280]{1,0:T(8,128)(2,1)} %bitcast.9, bf16[80,1536]{1,0:T(8,128)(2,1)} %bitcast.11), custom_call_target="tpu_custom_call" | custom-call | flops 9437184000 | bytes 16384000 | tf_op jit(solution)/shard_map/pallas_call | solution.py:555
  71.4 0.0 copy-start
  71.4 3.0 %convert_bitcast_fusion = f32[96,5,1280]{2,0,1:T(8,128)} fusion(bf16[5,96,1280]{2,1,0:T(8,128)(2,1)} %get-tuple-element.4), kind=kLoop, calls=%fused_computation | loop fusion | flops 614400 | bytes 3686400 | tf_op jit(solution)/shard_map/transpose | solution.py:603
  74.4 0.0 copy-done
  74.4 0.8 %copy.6 = bf16[1,320,640]{2,1,0:T(8,128)(2,1)} copy(bf16[1,320,640]{2,1,0:T(8,128)(2,1)S(1)} %bitcast.8) | data formatting | bytes 819200
Async XLA Ops:
  71.4 3.0 %copy-start = (bf16[320,640]{1,0:T(8,128)(2,1)S(1)}, bf16[320,640]{1,0:T(8,128)(2,1)}, u32[]{:S(2)}) copy-start(bf16[320,640]{1,0:T(8,128)(2,1)} %get-tuple-element.5) | copy-start | bytes 1228804
